TPU v7x, 32 devices: a whole 2x2x4 slice. The times are simulated.
32 devices in a mesh: groups: 2 (over y), section: 4 (over x, core), space: 4 (over z).
Axes of the slice: x: 2, y: 2, z: 4, core: 2. Of those that a mesh axis runs over, the one named last changes fastest.
Arguments:
- layer_inputs: bfloat16 [4, 8192, 512], P('section', ('groups', 'space')), parts along dimension 1, may hold values from -54 to 54
- saved_queries: bfloat16 [4, 128, 64, 512], P('section', ('groups', 'space')), parts along dimension 1, may hold values from -8 to 8
- saved_keys: bfloat16 [4, 128, 64, 512], P('section', ('groups', 'space')), parts along dimension 1, may hold values from -8 to 8
- value_weight: bfloat16 [4, 512, 512], P('section'), may hold values from -0.25 to 0.25
- out_weight: bfloat16 [4, 512, 512], P('section'), may hold values from -0.25 to 0.25
- norm_gain: bfloat16 [4, 512], P('section'), may hold values from 0.099609375 to 1.8984375
- cotangent: bfloat16 [8192, 512], P(('groups', 'space'), 'section'), parts along dimension 0, may hold values from -24 to 24
Outputs:
- input_grad: bfloat16 [8192, 512], P(('groups', 'space'), 'section'), parts along dimension 0
- value_grad: float32 [4, 1024, 512], P('section', ('groups', 'space')), parts along dimension 1
- out_grad: float32 [4, 1024, 512], P('section', ('groups', 'space')), parts along dimension 1
- gain_grad: float32 [4, 1024], P('section', 'groups'), parts along dimension 1
There are 2 independent parts, one for each index of `groups`. A program takes and returns all parts, laid end to end along the dimension named above; an argument that names none is the same for every part. Nothing has to cross between parts.
All inputs are finite; a program needn't handle non-finite values.
Results may differ from a plain program's by a relative error of at most 0.013.
Values may be sent and summed in bfloat16 or wider, within the bound.
A program may use at most 128 MiB of HBM per device.

v0:
```python
import functools

import jax
import jax.numpy as jnp
from jax import lax
from jax.experimental import pallas as pl
from jax.experimental.pallas import tpu as pltpu
from jax.sharding import PartitionSpec as P

HD = 32
COLS = 64


epsilon = 1e-06


def shifted(block, axis, distance):
    devices = range(lax.axis_size(axis))
    route = [(i - distance, i) for i in devices if i - distance in devices]
    return lax.ppermute(block, axis, route)


def to_pieces(rows_in, band, spaces):
    width = rows_in.shape[-1]
    blocks = rows_in.reshape(band // 8, 8, 8, COLS // 8, width).transpose(1, 3, 0, 2, 4)
    return blocks.reshape(spaces, COLS // spaces, band // 8, 8, width)


def from_pieces(pieces, band, spaces):
    width = pieces.shape[-1]
    depth = band // 8 * spaces // 8
    blocks = pieces.transpose(0, 2, 1, 3, 4).reshape(8, depth, COLS // spaces, 8, width)
    return blocks.transpose(1, 2, 0, 3, 4).reshape(-1, width)


def to_window_pieces(rows_in, band, spaces):
    width = rows_in.shape[-1]
    depth = band // 8 * spaces // 8
    blocks = rows_in.reshape(depth, COLS // spaces, 8, 8, width).transpose(2, 0, 1, 3, 4)
    return blocks.reshape(spaces, band // 8, COLS // spaces, 8, width).transpose(0, 2, 1, 3, 4)


def from_window_pieces(pieces, band):
    width = pieces.shape[-1]
    blocks = pieces.reshape(8, COLS // 8, band // 8, 8, width).transpose(2, 0, 3, 1, 4)
    return blocks.reshape(-1, width)


def window_probs(queries, keys_in):
    count = queries.shape[0]
    heads = queries.shape[-1] // HD
    qv = queries.reshape(count, 64, heads, HD)
    kv = keys_in.reshape(count, 64, heads, HD)
    scores = jnp.einsum("wqhd,wkhd->whqk", qv, kv, preferred_element_type=jnp.float32) * HD ** (
        -0.5
    )
    return jax.nn.softmax(scores, axis=-1).astype(jnp.bfloat16)


def attend(probs, values):
    count = probs.shape[0]
    heads = probs.shape[1]
    grid = values.reshape(count, 64, heads, -1)
    out = jnp.einsum("whqk,wkhd->wqhd", probs, grid, preferred_element_type=jnp.float32)
    return out.reshape(count * 64, -1).astype(jnp.bfloat16)


def attend_back(probs, grads):
    count = probs.shape[0]
    heads = probs.shape[1]
    grid = grads.reshape(count, 64, heads, -1)
    out = jnp.einsum("whqk,wqhd->wkhd", probs, grid, preferred_element_type=jnp.float32)
    return out.reshape(count * 64, -1).astype(jnp.bfloat16)


def inverse_rms(values):
    floats = values.astype(jnp.float32)
    return 1.0 / jnp.sqrt(jnp.mean(floats * floats, axis=-1, keepdims=True) + epsilon)


def local_plain(layer_inputs, saved_queries, saved_keys, value_weight, out_weight, norm_gain, cotangent):
    sections = lax.axis_size("section")
    spaces = lax.axis_size("space")
    section_index = lax.axis_index("section")
    inputs = layer_inputs[0]
    w_value = value_weight[0]
    w_out = out_weight[0]
    gains = norm_gain[0].astype(jnp.float32)
    tok_rows = inputs.shape[0]
    width = inputs.shape[1]
    band = tok_rows // COLS
    factor = float(tok_rows * spaces) ** (-0.5)
    probs = window_probs(saved_queries[0], saved_keys[0])

    def exchange(block):
        return lax.all_to_all(block, "space", split_axis=0, concat_axis=0, tiled=True)

    def to_windows(rows_in):
        return from_pieces(exchange(to_pieces(rows_in, band, spaces)), band, spaces)

    def to_bands(rows_in):
        return from_window_pieces(exchange(to_window_pieces(rows_in, band, spaces)), band)

    cot = lax.all_gather(to_windows(cotangent), "section", axis=1, tiled=True)
    inputs = to_windows(inputs)
    rstd = inverse_rms(inputs)
    normed = inputs.astype(jnp.float32) * rstd
    hidden = (normed * gains).astype(jnp.bfloat16)
    values = jnp.dot(hidden, w_value, preferred_element_type=jnp.float32).astype(jnp.bfloat16)
    attended = attend(probs, values)
    keep_values = jnp.zeros((tok_rows, w_value.shape[1]), jnp.bfloat16)
    keep_cot = jnp.zeros((tok_rows, width), jnp.bfloat16)
    result = cot
    for layer_step in range(sections):
        grad_attn = jnp.dot(cot, w_out, preferred_element_type=jnp.float32).astype(jnp.bfloat16)
        grad_values = attend_back(probs, grad_attn)
        grad_norm = lax.dot_general(
            grad_values, w_value, (((1,), (1,)), ((), ())), preferred_element_type=jnp.float32
        )
        scaled = grad_norm * gains
        total = cot.astype(jnp.float32) + rstd * (
            scaled - normed * jnp.mean(scaled * normed, axis=-1, keepdims=True)
        )
        active = section_index == sections - 1 - layer_step
        keep_values = jnp.where(active, grad_values, keep_values)
        keep_cot = jnp.where(active, cot, keep_cot)
        result = total.astype(jnp.bfloat16)
        if layer_step + 1 < sections:
            cot = shifted(result, "section", -1)
    quarter = width // sections
    split = result.reshape(tok_rows, sections, quarter).transpose(1, 0, 2)
    mine = lax.all_to_all(split, "section", split_axis=0, concat_axis=0, tiled=True)[0]
    input_grad = to_bands(mine)
    kept_norm = lax.dot_general(
        keep_values, w_value, (((1,), (1,)), ((), ())), preferred_element_type=jnp.float32
    )
    gain_part = jnp.sum(kept_norm * normed, axis=0)
    first = lax.dot_general(
        hidden, keep_values, (((0,), (0,)), ((), ())), preferred_element_type=jnp.float32
    )
    second = lax.dot_general(
        keep_cot, attended, (((0,), (0,)), ((), ())), preferred_element_type=jnp.float32
    )
    totals = lax.psum_scatter(
        jnp.concatenate([first, second], axis=1) * factor, "space", scatter_dimension=0, tiled=True
    )
    channels = w_value.shape[1]
    value_grad = totals[:, :channels][None]
    out_grad = totals[:, channels:][None]
    gain_grad = lax.psum(gain_part * factor, "space")[None]
    return (input_grad, value_grad, out_grad, gain_grad)


MESH = pl.DeviceIdType.MESH
CHUNKS = 4
F32 = jnp.float32
BF16 = jnp.bfloat16


def dot(left, right, contract):
    return lax.dot_general(left, right, ((contract[:1], contract[1:]), ((), ())),
                           preferred_element_type=F32)


def fused(sections, spaces, reps, factor,
          x_ref, q_ref, k_ref, wv_ref, wo_ref, gain_ref, cot_ref,
          ig_ref, vg_ref, og_ref, gg_ref,
          xs, xr, cs, cr, ch, res, pt, vacc, oacc, gacc, iso, iri, ws, wr, gr,
          x_ss, x_rs, c_ss, c_rs, h_ss, h_rs, i_ss, i_rs, w_ss, w_rs, g_ss, g_rs):
    sec = lax.axis_index("section")
    z = lax.axis_index("space")
    last = sections - 1
    tile = reps * 8
    windows = q_ref.shape[0]
    wc = windows // CHUNKS
    rows = wc * 64
    crow = wc * tile
    width = x_ref.shape[1]
    quarter = cot_ref.shape[1]
    groups = width // 128

    def dev(s, zz):
        return {"section": s, "space": zz}

    def around(pos, step, size):
        return lax.rem(pos + step, size)

    def remote(src, dst, ssem, rsem, target):
        return pltpu.make_async_remote_copy(
            src_ref=src, dst_ref=dst, send_sem=ssem, recv_sem=rsem,
            device_id=target, device_id_type=MESH)

    barrier = pltpu.get_barrier_semaphore()
    for a in range(sections):
        for b in range(spaces):
            if a or b:
                pl.semaphore_signal(
                    barrier, inc=1,
                    device_id=dev(around(sec, a, sections), around(z, b, spaces)),
                    device_id_type=MESH)

    size = reps * 64
    shift = tile.bit_length() - 1
    row_at = lax.broadcasted_iota(jnp.int32, (size, size), 0)
    col_at = lax.broadcasted_iota(jnp.int32, (size, size), 1)
    wanted = (((row_at >> 3) & (reps - 1)) << 6) + ((row_at & 7) << 3) + (row_at >> shift)
    perm = jnp.where(wanted == col_at, 1.0, 0.0).astype(BF16)
    blocks = size // crow

    def reorder(y0, ref):
        parts = [ref[pl.ds(pl.multiple_of(r * 512 + y0 * 64, 64), 64), :] for r in range(reps)]
        return dot(perm, jnp.concatenate(parts, axis=0), (1, 0)).astype(BF16)

    def split_cot(y0, carry):
        cs[pl.ds(y0 * blocks, blocks)] = reorder(y0, cot_ref).reshape(blocks, crow, quarter)
        return carry

    def split_x(y0, carry):
        xs[pl.ds(y0 * blocks, blocks)] = reorder(y0, x_ref).reshape(blocks, crow, width)
        return carry

    lax.fori_loop(0, 8, split_cot, 0)
    pl.semaphore_wait(barrier, sections * spaces - 1)

    def cot_copy(b):
        d = around(z, b, spaces)
        return remote(cs.at[pl.ds(d * CHUNKS, CHUNKS)], cr.at[sec, z], c_ss.at[b],
                      c_rs.at[sec * spaces + z], dev(last, d))

    for b in range(1, spaces):
        cot_copy(b).start()

    @pl.when(sec != last)
    def _():
        cot_copy(0).start()

    @pl.when(sec == last)
    def _():
        cr[last, z] = cs[pl.ds(z * CHUNKS, CHUNKS)]

    lax.fori_loop(0, 8, split_x, 0)

    def x_copy(p, c):
        d = around(z, p, spaces)
        return remote(xs.at[d * CHUNKS + c], xr.at[z * CHUNKS + c], x_ss.at[p * CHUNKS + c],
                      x_rs.at[z * CHUNKS + c], dev(sec, d))

    def start_x(c, carry):
        for p in range(1, spaces):
            x_copy(p, c).start()
        return carry

    lax.fori_loop(0, CHUNKS, start_x, 0)
    xr[pl.ds(z * CHUNKS, CHUNKS)] = xs[pl.ds(z * CHUNKS, CHUNKS)]

    lane = lax.broadcasted_iota(jnp.int32, (1, 128), 1)
    per = 128 // HD
    heads = [(lane >= h * HD) & (lane < h * HD + HD) for h in range(per)]
    masks = [jnp.where(m, 1.0, 0.0).astype(BF16) for m in heads]

    def spread(block):
        return jnp.concatenate([block * m for m in masks], axis=0)

    def make_probs(w, carry):
        for g in range(groups):
            at = slice(g * 128, g * 128 + 128)
            scores = dot(k_ref[w, :, at], spread(q_ref[w, :, at]), (1, 1)) * HD ** (-0.5)
            top = jnp.max(scores, axis=0, keepdims=True)
            powers = jnp.exp(scores - top)
            pt[w * groups + g] = (
                powers * (1.0 / jnp.sum(powers, axis=0, keepdims=True))).astype(BF16)
        return carry

    lax.fori_loop(0, windows, make_probs, 0)
    vacc[...] = jnp.zeros_like(vacc)
    oacc[...] = jnp.zeros_like(oacc)
    gacc[...] = jnp.zeros_like(gacc)

    def out_copy(c, a, b):
        d = around(z, b, spaces)
        return remote(iso.at[(c * sections + a) * spaces + d], iri.at[z * CHUNKS + c],
                      i_ss.at[(c * sections + a) * spaces + b], i_rs.at[z * CHUNKS + c],
                      dev(a, d))

    def chain_copy(c):
        return remote(res.at[c], ch.at[c], h_ss.at[c], h_rs.at[c],
                      dev(lax.rem(sec + last, sections), z))

    @pl.when(sec == last)
    def _():
        for a in range(sections):
            for b in range(spaces):
                src = around(z, b, spaces)

                def arrive(a=a, src=src):
                    remote(cs.at[pl.ds(0, CHUNKS)], cr.at[a, src], c_ss.at[0],
                           c_rs.at[a * spaces + src], dev(a, src)).wait_recv()

                if a != last or b != 0:
                    arrive()
        for c in range(CHUNKS):
            for a in range(sections):
                for u in range(wc):
                    ch[c, u * 64:u * 64 + 64, a * quarter:(a + 1) * quarter] = jnp.concatenate(
                        [cr[a, s, c, u * tile:(u + 1) * tile, :] for s in range(spaces)], axis=0)

    def step(c, carry):
        for p in range(1, spaces):
            src = around(z, p, spaces)
            remote(xs.at[0], xr.at[src * CHUNKS + c], x_ss.at[0], x_rs.at[src * CHUNKS + c],
                   dev(sec, src)).wait_recv()
        parts = [xr[s * CHUNKS + c, u * tile:(u + 1) * tile, :]
                 for u in range(wc) for s in range(spaces)]
        xf = jnp.concatenate(parts, axis=0).astype(F32)
        rstd = 1.0 / jnp.sqrt(jnp.mean(xf * xf, axis=-1, keepdims=True) + epsilon)
        normed = xf * rstd
        gains = gain_ref[...].astype(F32)
        hidden = (normed * gains).astype(BF16)
        values = dot(hidden, wv_ref[...], (1, 0)).astype(BF16)
        out_rows = []
        for w in range(wc):
            out_cols = []
            for g in range(groups):
                full = dot(pt[(c * wc + w) * groups + g],
                           values[w * 64:w * 64 + 64, g * 128:g * 128 + 128], (0, 0))
                one = jnp.where(heads[0], full[:64], 0.0)
                for h in range(1, per):
                    one = jnp.where(heads[h], full[h * 64:h * 64 + 64], one)
                out_cols.append(one.astype(BF16))
            out_rows.append(jnp.concatenate(out_cols, axis=1))
        attended = jnp.concatenate(out_rows, axis=0)

        @pl.when(sec != last)
        def _():
            chain_copy(c).wait_recv()

        cot = ch[c]
        grad_attn = dot(cot, wo_ref[...], (1, 0)).astype(BF16)
        out_rows = []
        for w in range(wc):
            out_cols = []
            for g in range(groups):
                out_cols.append(dot(
                    pt[(c * wc + w) * groups + g],
                    spread(grad_attn[w * 64:w * 64 + 64, g * 128:g * 128 + 128]),
                    (1, 0)).astype(BF16))
            out_rows.append(jnp.concatenate(out_cols, axis=1))
        grad_values = jnp.concatenate(out_rows, axis=0)
        grad_norm = dot(grad_values, wv_ref[...], (1, 1))
        product = grad_norm * normed
        mean = jnp.mean(product * gains, axis=-1, keepdims=True)
        total = cot.astype(F32) + rstd * (grad_norm * gains - normed * mean)
        res[c] = total.astype(BF16)

        @pl.when(sec != 0)
        def _():
            chain_copy(c).start()

        @pl.when(sec == 0)
        def _():
            for a in range(sections):
                for s in range(spaces):
                    iso[(c * sections + a) * spaces + s] = jnp.concatenate(
                        [res[c, u * 64 + s * tile:u * 64 + (s + 1) * tile,
                             a * quarter:(a + 1) * quarter] for u in range(wc)], axis=0)
            for a in range(sections):
                for b in range(spaces):
                    if a or b:
                        out_copy(c, a, b).start()
            iri[z * CHUNKS + c] = iso[c * sections * spaces + z]

        gacc[...] += jnp.sum(product, axis=0, keepdims=True)
        oacc[...] += dot(cot, attended, (0, 0))
        vacc[...] += dot(hidden, grad_values, (0, 0))
        return carry

    lax.fori_loop(0, CHUNKS, step, 0)

    part = vg_ref.shape[0]
    for d in range(spaces):
        ws[d, 0] = (vacc[d * part:(d + 1) * part, :] * factor).astype(BF16)
        ws[d, 1] = (oacc[d * part:(d + 1) * part, :] * factor).astype(BF16)
    gacc[...] = gacc[...] * factor

    def w_copy(p):
        d = around(z, p, spaces)
        return remote(ws.at[d], wr.at[z], w_ss.at[p], w_rs.at[z], dev(sec, d))

    def g_copy(p):
        return remote(gacc, gr.at[z], g_ss.at[p], g_rs.at[z], dev(sec, around(z, p, spaces)))

    for p in range(1, spaces):
        g_copy(p).start()
        w_copy(p).start()

    for b in range(spaces):
        src = around(z, b, spaces)

        def pieces(src=src):
            for c in range(CHUNKS):
                remote(iso.at[0], iri.at[src * CHUNKS + c], i_ss.at[0],
                       i_rs.at[src * CHUNKS + c], dev(0, src)).wait_recv()

        if b:
            pieces()
        else:
            pl.when(sec != 0)(pieces)

    def join(y0, carry):
        block = iri[pl.ds(y0 * blocks, blocks)].reshape(size, quarter)
        moved = dot(perm, block, (0, 0)).astype(BF16)
        for r in range(reps):
            ig_ref[pl.ds(pl.multiple_of(r * 512 + y0 * 64, 64), 64), :] = (
                moved[r * 64:r * 64 + 64])
        return carry

    lax.fori_loop(0, 8, join, 0)

    own = pl.ds(pl.multiple_of(z * part, part), part)
    v_sum = vacc[own, :] * factor
    o_sum = oacc[own, :] * factor
    g_sum = gacc[...]
    for p in range(1, spaces):
        src = around(z, p, spaces)
        remote(gacc, gr.at[src], g_ss.at[0], g_rs.at[src], dev(sec, src)).wait_recv()
        remote(ws.at[0], wr.at[src], w_ss.at[0], w_rs.at[src], dev(sec, src)).wait_recv()
        v_sum += wr[src, 0].astype(F32)
        o_sum += wr[src, 1].astype(F32)
        g_sum += gr[src]
    vg_ref[...] = v_sum
    og_ref[...] = o_sum
    gg_ref[...] = g_sum[0:1]

    for p in range(1, spaces):
        g_copy(p).wait_send()
        w_copy(p).wait_send()
        cot_copy(p).wait_send()

    def sent_x(c, carry):
        for p in range(1, spaces):
            x_copy(p, c).wait_send()
        return carry

    lax.fori_loop(0, CHUNKS, sent_x, 0)

    @pl.when(sec != last)
    def _():
        cot_copy(0).wait_send()

    def sent(c, carry):
        @pl.when(sec != 0)
        def _():
            chain_copy(c).wait_send()

        @pl.when(sec == 0)
        def _():
            for a in range(sections):
                for b in range(spaces):
                    if a or b:
                        out_copy(c, a, b).wait_send()
        return carry

    lax.fori_loop(0, CHUNKS, sent, 0)


def fused_call(x, q, k, wv, wo, gain, cot):
    sections = lax.axis_size("section")
    spaces = lax.axis_size("space")
    tok, width = x.shape
    quarter = cot.shape[1]
    reps = tok // COLS // 8
    windows = q.shape[0]
    crow = windows // CHUNKS * reps * 8
    rows = windows // CHUNKS * 64
    part = width // spaces
    factor = float(tok * spaces) ** (-0.5)
    dma = lambda n: pltpu.SemaphoreType.DMA((n,))
    vmem = lambda *shape: pltpu.VMEM(shape, BF16)
    fmem = lambda *shape: pltpu.VMEM(shape, F32)
    sc = spaces * CHUNKS
    full = sections * sc
    return pl.pallas_call(
        functools.partial(fused, sections, spaces, reps, factor),
        out_shape=(
            jax.ShapeDtypeStruct((tok, quarter), BF16),
            jax.ShapeDtypeStruct((part, width), F32),
            jax.ShapeDtypeStruct((part, width), F32),
            jax.ShapeDtypeStruct((1, width), F32),
        ),
        in_specs=[pl.BlockSpec(memory_space=pltpu.VMEM)] * 7,
        out_specs=[pl.BlockSpec(memory_space=pltpu.VMEM)] * 4,
        scratch_shapes=[
            vmem(sc, crow, width), vmem(sc, crow, width),
            vmem(sc, crow, quarter), vmem(sections, spaces, CHUNKS, crow, quarter),
            vmem(CHUNKS, rows, width), vmem(CHUNKS, rows, width),
            vmem(windows * (width // 128), 64, 64 * (128 // HD)),
            fmem(width, width), fmem(width, width), fmem(8, width),
            vmem(full, crow, quarter), vmem(sc, crow, quarter),
            vmem(spaces, 2, part, width), vmem(spaces, 2, part, width),
            fmem(spaces, 8, width),
            dma(sc), dma(sc), dma(spaces), dma(sections * spaces), dma(CHUNKS), dma(CHUNKS),
            dma(full), dma(sc), dma(spaces), dma(spaces), dma(spaces), dma(spaces),
        ],
        compiler_params=pltpu.CompilerParams(
            collective_id=0, has_side_effects=True, vmem_limit_bytes=50 * 2**20),
        cost_estimate=pl.CostEstimate(
            flops=2 * tok * width * width * 5, bytes_accessed=16 * tok * width,
            transcendentals=windows * 64 * 64 * (width // HD)),
    )(x, q, k, wv, wo, gain, cot)


def local(layer_inputs, saved_queries, saved_keys, value_weight, out_weight, norm_gain, cotangent):
    spaces = lax.axis_size("space")
    tok, width = layer_inputs.shape[1:]
    reps = tok // COLS // 8
    fits = (
        reps * 8 * COLS == tok and reps * spaces == 8 and reps >= 2
        and saved_queries.shape[1] % CHUNKS == 0 and cotangent.shape[1] % 128 == 0
        and value_weight.shape[1] == value_weight.shape[2] and width % (128 * spaces) == 0
    )
    if not fits:
        return local_plain(layer_inputs, saved_queries, saved_keys, value_weight, out_weight,
                           norm_gain, cotangent)
    input_grad, value_grad, out_grad, gain_grad = fused_call(
        layer_inputs[0], saved_queries[0], saved_keys[0], value_weight[0], out_weight[0],
        norm_gain, cotangent)
    return (input_grad, value_grad[None], out_grad[None], gain_grad)


def solution(mesh):
    in_specs = (
        P("section", ("groups", "space"), None),
        P("section", ("groups", "space"), None, None),
        P("section", ("groups", "space"), None, None),
        P("section", None, None),
        P("section", None, None),
        P("section", None),
        P(("groups", "space"), "section"),
    )
    out_specs = (
        P(("groups", "space"), "section"),
        P("section", ("groups", "space"), None),
        P("section", ("groups", "space"), None),
        P("section", "groups"),
    )
    return jax.shard_map(local, mesh=mesh, in_specs=in_specs, out_specs=out_specs, check_vma=False)
```

profile of v0, /device:TPU:0, one launch (start us, length us, event | category | flops | bytes accessed | tf_op | source)
XLA Modules:
  0.0 83.1 jit_solution(17985880117068808318)
XLA Ops:
  0.6 0.0 copy-start.4
  0.6 0.7 copy-done.4
  1.3 0.0 copy-start
  1.3 1.2 %copy-done = bf16[1,1024,512]{2,1,0:T(8,128)(2,1)S(1)} copy-done((bf16[1,1024,512]{2,1,0:T(8,128)(2,1)S(1)}, bf16[1,1024,512]{2,1,0:T(8,128)(2,1)}, u32[]{:S(2)}) %copy-start) | copy-done | bytes 1048600
  2.5 0.0 copy-start.1
  2.5 1.0 %copy-done.1 = bf16[1,512,512]{2,1,0:T(8,128)(2,1)S(1)} copy-done((bf16[1,512,512]{2,1,0:T(8,128)(2,1)S(1)}, bf16[1,512,512]{2,1,0:T(8,128)(2,1)}, u32[]{:S(2)}) %copy-start.1) | copy-done | bytes 524312
  3.6 0.0 copy-start.2
  3.6 1.0 %copy-done.2 = bf16[1,512,512]{2,1,0:T(8,128)(2,1)S(1)} copy-done((bf16[1,512,512]{2,1,0:T(8,128)(2,1)S(1)}, bf16[1,512,512]{2,1,0:T(8,128)(2,1)}, u32[]{:S(2)}) %copy-start.2) | copy-done | bytes 524312
  4.6 0.0 copy-start.3
  4.6 0.9 %copy-done.3 = bf16[1024,128]{1,0:T(8,128)(2,1)S(1)} copy-done((bf16[1024,128]{1,0:T(8,128)(2,1)S(1)}, bf16[1024,128]{1,0:T(8,128)(2,1)}, u32[]{:S(2)}) %copy-start.3) | copy-done | bytes 262168
  5.6 74.9 %shard_map.102 = (bf16[1024,128]{1,0:T(8,128)(2,1)S(1)}, f32[128,512]{1,0:T(8,128)S(1)}, f32[128,512]{1,0:T(8,128)S(1)}, f32[1,512]{1,0:T(1,128)S(1)}) custom-call(bf16[1024,512]{1,0:T(8,128)(2,1)S(1)} %bitcast.9, bf16[16,64,512]{2,1,0:T(8,128)(2,1)} %bitcast.12, bf16[16,64,512]{2,1,0:T(8,128)(2,1)} %bitcast.13, bf16[512,512]{1,0:T(8,128)(2,1)S(1)} %bitcast.10, ...), custom_call_target="tpu_custom_call" | custom-call | flops 2684354560 | bytes 8388608 | tf_op jit(solution)/shard_map/pallas_call | solution.py:482
  80.4 0.7 copy.15
  81.2 0.7 copy.16
  81.9 0.7 copy.17
  82.6 0.6 copy.18
Async XLA Ops:
  0.6 0.7 copy-start.4
  1.3 1.2 %copy-start = (bf16[1,1024,512]{2,1,0:T(8,128)(2,1)S(1)}, bf16[1,1024,512]{2,1,0:T(8,128)(2,1)}, u32[]{:S(2)}) copy-start(bf16[1,1024,512]{2,1,0:T(8,128)(2,1)} %param.7) | copy-start | bytes 3145732
  2.5 1.0 %copy-start.1 = (bf16[1,512,512]{2,1,0:T(8,128)(2,1)S(1)}, bf16[1,512,512]{2,1,0:T(8,128)(2,1)}, u32[]{:S(2)}) copy-start(bf16[1,512,512]{2,1,0:T(8,128)(2,1)} %param.10) | copy-start | bytes 1572868
  3.6 1.0 %copy-start.2 = (bf16[1,512,512]{2,1,0:T(8,128)(2,1)S(1)}, bf16[1,512,512]{2,1,0:T(8,128)(2,1)}, u32[]{:S(2)}) copy-start(bf16[1,512,512]{2,1,0:T(8,128)(2,1)} %param.11) | copy-start | bytes 1572868
  4.6 0.9 %copy-start.3 = (bf16[1024,128]{1,0:T(8,128)(2,1)S(1)}, bf16[1024,128]{1,0:T(8,128)(2,1)}, u32[]{:S(2)}) copy-start(bf16[1024,128]{1,0:T(8,128)(2,1)} %cot_ref.1) | copy-start | bytes 786436
where the time goes:
time: 84.5 us; the launch traced here: 83.1 us
  Pallas kernels  74.9 us (89%)
  local copies, waits for them, and re-layouts  7.62 us (9%)
    pallas_call x1, Pallas kernels, fused_call(): pl.pallas_call(functools.partial(fused, sections, spaces, reps, factor),...  74.9 us
    unnamed x14, local copies, waits for them, and re-layouts  7.62 us

commit v1 on v0

--- a/solution.py
+++ b/solution.py
@@ -153,6 +153,7 @@
 
 MESH = pl.DeviceIdType.MESH
 CHUNKS = 4
+AHEAD = 2
 F32 = jnp.float32
 BF16 = jnp.bfloat16
 
@@ -163,8 +164,9 @@
 
 
 def fused(sections, spaces, reps, factor,
-          x_ref, q_ref, k_ref, wv_ref, wo_ref, gain_ref, cot_ref,
+          x_in, q_in, k_in, wv_in, wo_in, gain_ref, cot_in,
           ig_ref, vg_ref, og_ref, gg_ref,
+          cot_ref, x_ref, q_ref, k_ref, wv_ref, wo_ref, l_s,
           xs, xr, cs, cr, ch, res, pt, vacc, oacc, gacc, iso, iri, ws, wr, gr,
           x_ss, x_rs, c_ss, c_rs, h_ss, h_rs, i_ss, i_rs, w_ss, w_rs, g_ss, g_rs):
     sec = lax.axis_index("section")
@@ -190,6 +192,13 @@
             src_ref=src, dst_ref=dst, send_sem=ssem, recv_sem=rsem,
             device_id=target, device_id_type=MESH)
 
+    def load(i):
+        src = (cot_in, x_in, q_in, k_in, wv_in, wo_in)[i]
+        dst = (cot_ref, x_ref, q_ref, k_ref, wv_ref, wo_ref)[i]
+        return pltpu.make_async_copy(src, dst, l_s.at[i])
+
+    for i in range(6):
+        load(i).start()
     barrier = pltpu.get_barrier_semaphore()
     for a in range(sections):
         for b in range(spaces):
@@ -219,7 +228,8 @@
         xs[pl.ds(y0 * blocks, blocks)] = reorder(y0, x_ref).reshape(blocks, crow, width)
         return carry
 
-    lax.fori_loop(0, 8, split_cot, 0)
+    load(0).wait()
+    lax.fori_loop(0, 8, split_cot, 0, unroll=4)
     pl.semaphore_wait(barrier, sections * spaces - 1)
 
     def cot_copy(b):
@@ -238,7 +248,8 @@
     def _():
         cr[last, z] = cs[pl.ds(z * CHUNKS, CHUNKS)]
 
-    lax.fori_loop(0, 8, split_x, 0)
+    load(1).wait()
+    lax.fori_loop(0, 8, split_x, 0, unroll=4)
 
     def x_copy(p, c):
         d = around(z, p, spaces)
@@ -250,7 +261,12 @@
             x_copy(p, c).start()
         return carry
 
-    lax.fori_loop(0, CHUNKS, start_x, 0)
+    early = lax.rem(sec, 2) == 1
+
+    @pl.when(early)
+    def _():
+        lax.fori_loop(0, AHEAD, start_x, 0)
+
     xr[pl.ds(z * CHUNKS, CHUNKS)] = xs[pl.ds(z * CHUNKS, CHUNKS)]
 
     lane = lax.broadcasted_iota(jnp.int32, (1, 128), 1)
@@ -271,7 +287,16 @@
                 powers * (1.0 / jnp.sum(powers, axis=0, keepdims=True))).astype(BF16)
         return carry
 
-    lax.fori_loop(0, windows, make_probs, 0)
+    load(2).wait()
+    load(3).wait()
+    lax.fori_loop(0, windows, make_probs, 0, unroll=2)
+
+    @pl.when(jnp.logical_not(early))
+    def _():
+        lax.fori_loop(0, AHEAD, start_x, 0)
+
+    load(4).wait()
+    load(5).wait()
     vacc[...] = jnp.zeros_like(vacc)
     oacc[...] = jnp.zeros_like(oacc)
     gacc[...] = jnp.zeros_like(gacc)
@@ -309,6 +334,11 @@
             src = around(z, p, spaces)
             remote(xs.at[0], xr.at[src * CHUNKS + c], x_ss.at[0], x_rs.at[src * CHUNKS + c],
                    dev(sec, src)).wait_recv()
+
+        @pl.when(c + AHEAD < CHUNKS)
+        def _():
+            start_x(c + AHEAD, 0)
+
         parts = [xr[s * CHUNKS + c, u * tile:(u + 1) * tile, :]
                  for u in range(wc) for s in range(spaces)]
         xf = jnp.concatenate(parts, axis=0).astype(F32)
@@ -414,7 +444,7 @@
                 moved[r * 64:r * 64 + 64])
         return carry
 
-    lax.fori_loop(0, 8, join, 0)
+    lax.fori_loop(0, 8, join, 0, unroll=4)
 
     own = pl.ds(pl.multiple_of(z * part, part), part)
     v_sum = vacc[own, :] * factor
@@ -487,9 +517,11 @@
             jax.ShapeDtypeStruct((part, width), F32),
             jax.ShapeDtypeStruct((1, width), F32),
         ),
-        in_specs=[pl.BlockSpec(memory_space=pltpu.VMEM)] * 7,
+        in_specs=[pl.BlockSpec(memory_space=pltpu.VMEM if i == 5 else pltpu.HBM) for i in range(7)],
         out_specs=[pl.BlockSpec(memory_space=pltpu.VMEM)] * 4,
         scratch_shapes=[
+            vmem(*cot.shape), vmem(*x.shape), vmem(*q.shape), vmem(*k.shape), vmem(*wv.shape),
+            vmem(*wo.shape), dma(6),
             vmem(sc, crow, width), vmem(sc, crow, width),
             vmem(sc, crow, quarter), vmem(sections, spaces, CHUNKS, crow, quarter),
             vmem(CHUNKS, rows, width), vmem(CHUNKS, rows, width),

time: 84.5 us -> 82.2 us (0.973)
  Pallas kernels: 74.9 us -> 73 us
    pallas_call x1, Pallas kernels: 74.9 us -> 73 us  [fused_call(): pl.pallas_call(functools.partial(fused, sections, spaces, reps, factor),...]
where the time goes in v1:
time: 82.2 us; the launch traced here: 81.3 us
  Pallas kernels  73 us (89%)
  local copies, waits for them, and re-layouts  7.62 us (9%)
    pallas_call x1, Pallas kernels, fused_call(): pl.pallas_call(functools.partial(fused, sections, spaces, reps, factor),...  73 us
    unnamed x14, local copies, waits for them, and re-layouts  7.62 us

profile of v1, /device:TPU:0, one launch (start us, length us, event | category | flops | bytes accessed | tf_op | source)
XLA Modules:
  0.0 81.3 jit_solution(7561699850394494154)
XLA Ops:
  0.6 0.0 copy-start.4
  0.6 0.7 copy-done.4
  1.3 0.0 copy-start
  1.3 1.2 %copy-done = bf16[1,1024,512]{2,1,0:T(8,128)(2,1)S(1)} copy-done((bf16[1,1024,512]{2,1,0:T(8,128)(2,1)S(1)}, bf16[1,1024,512]{2,1,0:T(8,128)(2,1)}, u32[]{:S(2)}) %copy-start) | copy-done | bytes 1048600
  2.5 0.0 copy-start.1
  2.5 1.0 %copy-done.1 = bf16[1,512,512]{2,1,0:T(8,128)(2,1)S(1)} copy-done((bf16[1,512,512]{2,1,0:T(8,128)(2,1)S(1)}, bf16[1,512,512]{2,1,0:T(8,128)(2,1)}, u32[]{:S(2)}) %copy-start.1) | copy-done | bytes 524312
  3.6 0.0 copy-start.2
  3.6 1.0 %copy-done.2 = bf16[1,512,512]{2,1,0:T(8,128)(2,1)S(1)} copy-done((bf16[1,512,512]{2,1,0:T(8,128)(2,1)S(1)}, bf16[1,512,512]{2,1,0:T(8,128)(2,1)}, u32[]{:S(2)}) %copy-start.2) | copy-done | bytes 524312
  4.6 0.0 copy-start.3
  4.6 0.9 %copy-done.3 = bf16[1024,128]{1,0:T(8,128)(2,1)S(1)} copy-done((bf16[1024,128]{1,0:T(8,128)(2,1)S(1)}, bf16[1024,128]{1,0:T(8,128)(2,1)}, u32[]{:S(2)}) %copy-start.3) | copy-done | bytes 262168
  5.6 73.0 %shard_map.102 = (bf16[1024,128]{1,0:T(8,128)(2,1)S(1)}, f32[128,512]{1,0:T(8,128)S(1)}, f32[128,512]{1,0:T(8,128)S(1)}, f32[1,512]{1,0:T(1,128)S(1)}) custom-call(bf16[1024,512]{1,0:T(8,128)(2,1)S(1)} %bitcast.9, bf16[16,64,512]{2,1,0:T(8,128)(2,1)} %bitcast.12, bf16[16,64,512]{2,1,0:T(8,128)(2,1)} %bitcast.13, bf16[512,512]{1,0:T(8,128)(2,1)S(1)} %bitcast.10, ...), custom_call_target="tpu_custom_call" | custom-call | flops 2684354560 | bytes 8388608 | tf_op jit(solution)/shard_map/pallas_call | solution.py:512
  78.6 0.7 copy.15
  79.3 0.7 copy.16
  80.0 0.7 copy.17
  80.7 0.6 copy.18
Async XLA Ops:
  0.6 0.7 copy-start.4
  1.3 1.2 %copy-start = (bf16[1,1024,512]{2,1,0:T(8,128)(2,1)S(1)}, bf16[1,1024,512]{2,1,0:T(8,128)(2,1)}, u32[]{:S(2)}) copy-start(bf16[1,1024,512]{2,1,0:T(8,128)(2,1)} %param.7) | copy-start | bytes 3145732
  2.5 1.0 %copy-start.1 = (bf16[1,512,512]{2,1,0:T(8,128)(2,1)S(1)}, bf16[1,512,512]{2,1,0:T(8,128)(2,1)}, u32[]{:S(2)}) copy-start(bf16[1,512,512]{2,1,0:T(8,128)(2,1)} %param.10) | copy-start | bytes 1572868
  3.6 1.0 %copy-start.2 = (bf16[1,512,512]{2,1,0:T(8,128)(2,1)S(1)}, bf16[1,512,512]{2,1,0:T(8,128)(2,1)}, u32[]{:S(2)}) copy-start(bf16[1,512,512]{2,1,0:T(8,128)(2,1)} %param.11) | copy-start | bytes 1572868
  4.6 0.9 %copy-start.3 = (bf16[1024,128]{1,0:T(8,128)(2,1)S(1)}, bf16[1024,128]{1,0:T(8,128)(2,1)}, u32[]{:S(2)}) copy-start(bf16[1024,128]{1,0:T(8,128)(2,1)} %cot_in.1) | copy-start | bytes 786436

commit v2 on v1

--- a/solution.py
+++ b/solution.py
@@ -407,9 +407,6 @@
     lax.fori_loop(0, CHUNKS, step, 0)
 
     part = vg_ref.shape[0]
-    for d in range(spaces):
-        ws[d, 0] = (vacc[d * part:(d + 1) * part, :] * factor).astype(BF16)
-        ws[d, 1] = (oacc[d * part:(d + 1) * part, :] * factor).astype(BF16)
     gacc[...] = gacc[...] * factor
 
     def w_copy(p):
@@ -420,8 +417,13 @@
         return remote(gacc, gr.at[z], g_ss.at[p], g_rs.at[z], dev(sec, around(z, p, spaces)))
 
     for p in range(1, spaces):
+        d = around(z, p, spaces)
+        rows_of = pl.ds(pl.multiple_of(d * part, part), part)
+        ws[d, 0] = (vacc[rows_of, :] * factor).astype(BF16)
+        ws[d, 1] = (oacc[rows_of, :] * factor).astype(BF16)
+        w_copy(p).start()
+    for p in range(1, spaces):
         g_copy(p).start()
-        w_copy(p).start()
 
     for b in range(spaces):
         src = around(z, b, spaces)

time: 82.2 us -> 84.4 us (1.027)
  Pallas kernels: 73 us -> 75.8 us
    pallas_call x1, Pallas kernels: 73 us -> 75.8 us  [fused_call(): pl.pallas_call(functools.partial(fused, sections, spaces, reps, factor),...]
where the time goes in v2:
time: 84.4 us; the launch traced here: 84.1 us
  Pallas kernels  75.8 us (90%)
  local copies, waits for them, and re-layouts  7.62 us (9%)
    pallas_call x1, Pallas kernels, fused_call(): pl.pallas_call(functools.partial(fused, sections, spaces, reps, factor),...  75.8 us
    unnamed x14, local copies, waits for them, and re-layouts  7.62 us

profile of v2, /device:TPU:0, one launch (start us, length us, event | category | flops | bytes accessed | tf_op | source)
XLA Modules:
  0.0 84.1 jit_solution(1736782172707496701)
XLA Ops:
  0.6 0.0 copy-start.4
  0.6 0.7 copy-done.4
  1.3 0.0 copy-start
  1.3 1.2 %copy-done = bf16[1,1024,512]{2,1,0:T(8,128)(2,1)S(1)} copy-done((bf16[1,1024,512]{2,1,0:T(8,128)(2,1)S(1)}, bf16[1,1024,512]{2,1,0:T(8,128)(2,1)}, u32[]{:S(2)}) %copy-start) | copy-done | bytes 1048600
  2.5 0.0 copy-start.1
  2.5 1.0 %copy-done.1 = bf16[1,512,512]{2,1,0:T(8,128)(2,1)S(1)} copy-done((bf16[1,512,512]{2,1,0:T(8,128)(2,1)S(1)}, bf16[1,512,512]{2,1,0:T(8,128)(2,1)}, u32[]{:S(2)}) %copy-start.1) | copy-done | bytes 524312
  3.6 0.0 copy-start.2
  3.6 1.0 %copy-done.2 = bf16[1,512,512]{2,1,0:T(8,128)(2,1)S(1)} copy-done((bf16[1,512,512]{2,1,0:T(8,128)(2,1)S(1)}, bf16[1,512,512]{2,1,0:T(8,128)(2,1)}, u32[]{:S(2)}) %copy-start.2) | copy-done | bytes 524312
  4.6 0.0 copy-start.3
  4.6 0.9 %copy-done.3 = bf16[1024,128]{1,0:T(8,128)(2,1)S(1)} copy-done((bf16[1024,128]{1,0:T(8,128)(2,1)S(1)}, bf16[1024,128]{1,0:T(8,128)(2,1)}, u32[]{:S(2)}) %copy-start.3) | copy-done | bytes 262168
  5.6 75.8 %shard_map.102 = (bf16[1024,128]{1,0:T(8,128)(2,1)S(1)}, f32[128,512]{1,0:T(8,128)S(1)}, f32[128,512]{1,0:T(8,128)S(1)}, f32[1,512]{1,0:T(1,128)S(1)}) custom-call(bf16[1024,512]{1,0:T(8,128)(2,1)S(1)} %bitcast.9, bf16[16,64,512]{2,1,0:T(8,128)(2,1)} %bitcast.12, bf16[16,64,512]{2,1,0:T(8,128)(2,1)} %bitcast.13, bf16[512,512]{1,0:T(8,128)(2,1)S(1)} %bitcast.10, ...), custom_call_target="tpu_custom_call" | custom-call | flops 2684354560 | bytes 8388608 | tf_op jit(solution)/shard_map/pallas_call | solution.py:514
  81.4 0.7 copy.15
  82.1 0.7 copy.16
  82.8 0.7 copy.17
  83.5 0.6 copy.18
Async XLA Ops:
  0.6 0.7 copy-start.4
  1.3 1.2 %copy-start = (bf16[1,1024,512]{2,1,0:T(8,128)(2,1)S(1)}, bf16[1,1024,512]{2,1,0:T(8,128)(2,1)}, u32[]{:S(2)}) copy-start(bf16[1,1024,512]{2,1,0:T(8,128)(2,1)} %param.7) | copy-start | bytes 3145732
  2.5 1.0 %copy-start.1 = (bf16[1,512,512]{2,1,0:T(8,128)(2,1)S(1)}, bf16[1,512,512]{2,1,0:T(8,128)(2,1)}, u32[]{:S(2)}) copy-start(bf16[1,512,512]{2,1,0:T(8,128)(2,1)} %param.10) | copy-start | bytes 1572868
  3.6 1.0 %copy-start.2 = (bf16[1,512,512]{2,1,0:T(8,128)(2,1)S(1)}, bf16[1,512,512]{2,1,0:T(8,128)(2,1)}, u32[]{:S(2)}) copy-start(bf16[1,512,512]{2,1,0:T(8,128)(2,1)} %param.11) | copy-start | bytes 1572868
  4.6 0.9 %copy-start.3 = (bf16[1024,128]{1,0:T(8,128)(2,1)S(1)}, bf16[1024,128]{1,0:T(8,128)(2,1)}, u32[]{:S(2)}) copy-start(bf16[1024,128]{1,0:T(8,128)(2,1)} %cot_in.1) | copy-start | bytes 786436
